TPU v7x, 128 devices: a whole 4x4x4 slice. The times are simulated.
128 devices in a mesh: layer: 16 (over y, z_lo, core), tile: 8 (over x, z_hi).
Axes of the slice: x: 4, y: 4, z: 4 (z_hi: 2, z_lo: 2; z = z_hi * 2 + z_lo), core: 2. Of those that a mesh axis runs over, the one named last changes fastest.
Arguments:
- incident: bfloat16 [4096, 128], P('tile'), may hold values from -6 to 6
- interface: bfloat16 [32, 4096, 4096], P('layer', 'tile'), may hold values from -0.09375 to 0.09375
- eigvec: bfloat16 [32, 4096, 4096], P('layer', 'tile'), may hold values from -0.09375 to 0.09375
- angle: float32 [32, 4096], P('layer'), may hold values from -3.140625 to 3.140625
- decay: float32 [32, 4096], P('layer'), may hold values from 0.002 to 0.15
Outputs:
- fields: bfloat16 [32, 4096, 512], P('layer', 'tile')
- leaving: float32 [32, 4096, 128], P('layer', 'tile')
All inputs are finite; a program needn't handle non-finite values.
Results may differ from a plain program's by a relative error of at most 0.035.
Values sent between devices are 32-bit elements; how exact they have to be, the bound alone decides.
No kernel may reach another device: no remote copies, remote signals or barrier semaphores. Data moves between devices by JAX's collectives and lax.ppermute only.
A program may use at most 128 MiB of HBM per device.

v0:
```python
import jax
import jax.numpy as jnp
from jax import lax
from jax.sharding import PartitionSpec as P

DEPTHS = 4


def shifted(x, axis, by):
    peers = lax.axis_size(axis)
    pairs = [(i, i + by) for i in range(peers) if 0 <= i + by < peers]
    return lax.ppermute(x, axis, pairs)


def rotate(block, angle_row, decay_row, frac):
    half = block.shape[1] // 2
    real_part = block[:, :half]
    imag_part = block[:, half:]
    scale = jnp.exp(-frac * decay_row)
    cosine = (scale * jnp.cos(frac * angle_row))[:, None]
    sine = (scale * jnp.sin(frac * angle_row))[:, None]
    return jnp.concatenate(
        [cosine * real_part - sine * imag_part, sine * real_part + cosine * imag_part], axis=1
    )


def advance(current, interface, angle, decay):
    fulls = []
    leaves = []
    for layer_num in range(interface.shape[0]):
        full = lax.all_gather(current, "tile", axis=0, tiled=True)
        fulls.append(full)
        phased = rotate(full, angle[layer_num], decay[layer_num], 1.0).astype(jnp.bfloat16)
        current = jnp.dot(interface[layer_num], phased, preferred_element_type=jnp.float32)
        leaves.append(current)
    return (jnp.stack(fulls), jnp.stack(leaves))


def on_device(incident, interface, eigvec, angle, decay):
    groups = lax.axis_size("layer")
    member = lax.axis_index("layer")
    layers_here = interface.shape[0]
    shard_rows = interface.shape[1]
    orders = interface.shape[2]
    width = incident.shape[1]
    start_amps = incident.astype(jnp.float32)
    store_full = jnp.zeros((layers_here, orders, width), jnp.float32)
    store_leave = jnp.zeros((layers_here, shard_rows, width), jnp.float32)
    inbox = jnp.where(member == 0, start_amps, jnp.zeros_like(start_amps))

    def step_whole(step, carry):
        inbox, store_full, store_leave = carry
        fulls, leaves = advance(inbox, interface, angle, decay)
        active = member == step
        store_full = jnp.where(active, fulls, store_full)
        store_leave = jnp.where(active, leaves, store_leave)
        received = shifted(leaves[layers_here - 1], "layer", 1)
        inbox = jnp.where(member == step + 1, received, inbox)
        return (inbox, store_full, store_leave)

    inbox, store_full, store_leave = lax.fori_loop(
        0, groups, step_whole, (inbox, store_full, store_leave)
    )
    fields = []
    for layer_num in range(layers_here):
        depth = jnp.concatenate(
            [
                rotate(
                    store_full[layer_num], angle[layer_num], decay[layer_num], step / DEPTHS
                ).astype(jnp.bfloat16)
                for step in range(DEPTHS)
            ],
            axis=1,
        )
        fields.append(
            jnp.dot(eigvec[layer_num], depth, preferred_element_type=jnp.float32).astype(
                jnp.bfloat16
            )
        )
    return (jnp.stack(fields), store_leave)


def solution(mesh):
    in_specs = (
        P("tile", None),
        P("layer", "tile", None),
        P("layer", "tile", None),
        P("layer", None),
        P("layer", None),
    )
    out_specs = (P("layer", "tile", None), P("layer", "tile", None))
    return jax.shard_map(
        on_device, mesh=mesh, in_specs=in_specs, out_specs=out_specs, check_vma=False
    )
```

profile of v0, /device:TPU:0, one launch (start us, length us, event | category | flops | bytes accessed | tf_op | source)
XLA Modules:
  0.0 2142.4 jit_solution(3400688796050703200)
XLA Ops:
  16.3 2101.5 %while.20 = (s32[]{:T(128)}, f32[512,128]{0,1:T(8,128)S(1)}, f32[2,4096,128]{1,2,0:T(8,128)}, f32[2,512,128]{1,2,0:T(8,128)S(1)}, s32[]{:T(128)}, /*index=5*/f32...) while((s32[]{:T(128)}, f32[512,128]{0,1:T(8,128)S(1)}, ...), condition=%wide.region_1.2_spmd.clone, body=%wide.region_0.1_spmd.clone.sunk | while | flops 1085759488 | bytes 101220824 | solution.py:61
  18.1 59.5 %all-gather.3.cloned.1.call-done = f32[4096,128]{0,1:T(8,128)} async-done(((f32[512,128]{0,1:T(8,128)}), f32[4096,128]{0,1:T(8,128)}) %all-gather.3.cloned.1.call-update) | async-done | bytes 2097168 | tf_op jit(solution)/shard_map/while/body/eval_jaxpr/all_gather | solution.py:31
  79.3 4.5 fusion.65
  83.8 53.7 %all-gather.5.cloned.1.call-done = f32[4096,128]{0,1:T(8,128)} async-done(((f32[512,128]{0,1:T(8,128)}), f32[4096,128]{0,1:T(8,128)}) %all-gather.5.cloned.1.call-update) | async-done | bytes 2097168 | tf_op jit(solution)/shard_map/while/body/eval_jaxpr/all_gather | solution.py:31
  149.7 59.2 %all-gather.3.cloned.1.call-done = f32[4096,128]{0,1:T(8,128)} async-done(((f32[512,128]{0,1:T(8,128)}), f32[4096,128]{0,1:T(8,128)}) %all-gather.3.cloned.1.call-update) | async-done | bytes 2097168 | tf_op jit(solution)/shard_map/while/body/eval_jaxpr/all_gather | solution.py:31
  210.7 4.5 fusion.65
  215.2 53.7 %all-gather.5.cloned.1.call-done = f32[4096,128]{0,1:T(8,128)} async-done(((f32[512,128]{0,1:T(8,128)}), f32[4096,128]{0,1:T(8,128)}) %all-gather.5.cloned.1.call-update) | async-done | bytes 2097168 | tf_op jit(solution)/shard_map/while/body/eval_jaxpr/all_gather | solution.py:31
  281.1 58.8 %all-gather.3.cloned.1.call-done = f32[4096,128]{0,1:T(8,128)} async-done(((f32[512,128]{0,1:T(8,128)}), f32[4096,128]{0,1:T(8,128)}) %all-gather.3.cloned.1.call-update) | async-done | bytes 2097168 | tf_op jit(solution)/shard_map/while/body/eval_jaxpr/all_gather | solution.py:31
  341.8 4.5 fusion.65
  346.3 53.6 %all-gather.5.cloned.1.call-done = f32[4096,128]{0,1:T(8,128)} async-done(((f32[512,128]{0,1:T(8,128)}), f32[4096,128]{0,1:T(8,128)}) %all-gather.5.cloned.1.call-update) | async-done | bytes 2097168 | tf_op jit(solution)/shard_map/while/body/eval_jaxpr/all_gather | solution.py:31
  412.2 59.2 %all-gather.3.cloned.1.call-done = f32[4096,128]{0,1:T(8,128)} async-done(((f32[512,128]{0,1:T(8,128)}), f32[4096,128]{0,1:T(8,128)}) %all-gather.3.cloned.1.call-update) | async-done | bytes 2097168 | tf_op jit(solution)/shard_map/while/body/eval_jaxpr/all_gather | solution.py:31
  473.2 4.5 fusion.65
  477.7 53.7 %all-gather.5.cloned.1.call-done = f32[4096,128]{0,1:T(8,128)} async-done(((f32[512,128]{0,1:T(8,128)}), f32[4096,128]{0,1:T(8,128)}) %all-gather.5.cloned.1.call-update) | async-done | bytes 2097168 | tf_op jit(solution)/shard_map/while/body/eval_jaxpr/all_gather | solution.py:31
  543.6 59.2 %all-gather.3.cloned.1.call-done = f32[4096,128]{0,1:T(8,128)} async-done(((f32[512,128]{0,1:T(8,128)}), f32[4096,128]{0,1:T(8,128)}) %all-gather.3.cloned.1.call-update) | async-done | bytes 2097168 | tf_op jit(solution)/shard_map/while/body/eval_jaxpr/all_gather | solution.py:31
  604.6 4.5 fusion.65
  609.1 53.7 %all-gather.5.cloned.1.call-done = f32[4096,128]{0,1:T(8,128)} async-done(((f32[512,128]{0,1:T(8,128)}), f32[4096,128]{0,1:T(8,128)}) %all-gather.5.cloned.1.call-update) | async-done | bytes 2097168 | tf_op jit(solution)/shard_map/while/body/eval_jaxpr/all_gather | solution.py:31
  675.0 59.2 %all-gather.3.cloned.1.call-done = f32[4096,128]{0,1:T(8,128)} async-done(((f32[512,128]{0,1:T(8,128)}), f32[4096,128]{0,1:T(8,128)}) %all-gather.3.cloned.1.call-update) | async-done | bytes 2097168 | tf_op jit(solution)/shard_map/while/body/eval_jaxpr/all_gather | solution.py:31
  736.0 4.5 fusion.65
  740.5 53.6 %all-gather.5.cloned.1.call-done = f32[4096,128]{0,1:T(8,128)} async-done(((f32[512,128]{0,1:T(8,128)}), f32[4096,128]{0,1:T(8,128)}) %all-gather.5.cloned.1.call-update) | async-done | bytes 2097168 | tf_op jit(solution)/shard_map/while/body/eval_jaxpr/all_gather | solution.py:31
  806.4 59.2 %all-gather.3.cloned.1.call-done = f32[4096,128]{0,1:T(8,128)} async-done(((f32[512,128]{0,1:T(8,128)}), f32[4096,128]{0,1:T(8,128)}) %all-gather.3.cloned.1.call-update) | async-done | bytes 2097168 | tf_op jit(solution)/shard_map/while/body/eval_jaxpr/all_gather | solution.py:31
  867.4 4.5 fusion.65
  871.9 53.7 %all-gather.5.cloned.1.call-done = f32[4096,128]{0,1:T(8,128)} async-done(((f32[512,128]{0,1:T(8,128)}), f32[4096,128]{0,1:T(8,128)}) %all-gather.5.cloned.1.call-update) | async-done | bytes 2097168 | tf_op jit(solution)/shard_map/while/body/eval_jaxpr/all_gather | solution.py:31
  937.8 58.9 %all-gather.3.cloned.1.call-done = f32[4096,128]{0,1:T(8,128)} async-done(((f32[512,128]{0,1:T(8,128)}), f32[4096,128]{0,1:T(8,128)}) %all-gather.3.cloned.1.call-update) | async-done | bytes 2097168 | tf_op jit(solution)/shard_map/while/body/eval_jaxpr/all_gather | solution.py:31
  998.5 4.5 fusion.65
  1003.0 53.7 %all-gather.5.cloned.1.call-done = f32[4096,128]{0,1:T(8,128)} async-done(((f32[512,128]{0,1:T(8,128)}), f32[4096,128]{0,1:T(8,128)}) %all-gather.5.cloned.1.call-update) | async-done | bytes 2097168 | tf_op jit(solution)/shard_map/while/body/eval_jaxpr/all_gather | solution.py:31
  1068.9 58.9 %all-gather.3.cloned.1.call-done = f32[4096,128]{0,1:T(8,128)} async-done(((f32[512,128]{0,1:T(8,128)}), f32[4096,128]{0,1:T(8,128)}) %all-gather.3.cloned.1.call-update) | async-done | bytes 2097168 | tf_op jit(solution)/shard_map/while/body/eval_jaxpr/all_gather | solution.py:31
  1134.1 53.7 %all-gather.5.cloned.1.call-done = f32[4096,128]{0,1:T(8,128)} async-done(((f32[512,128]{0,1:T(8,128)}), f32[4096,128]{0,1:T(8,128)}) %all-gather.5.cloned.1.call-update) | async-done | bytes 2097168 | tf_op jit(solution)/shard_map/while/body/eval_jaxpr/all_gather | solution.py:31
  1200.0 59.2 %all-gather.3.cloned.1.call-done = f32[4096,128]{0,1:T(8,128)} async-done(((f32[512,128]{0,1:T(8,128)}), f32[4096,128]{0,1:T(8,128)}) %all-gather.3.cloned.1.call-update) | async-done | bytes 2097168 | tf_op jit(solution)/shard_map/while/body/eval_jaxpr/all_gather | solution.py:31
  1261.0 4.5 fusion.65
  1265.5 53.7 %all-gather.5.cloned.1.call-done = f32[4096,128]{0,1:T(8,128)} async-done(((f32[512,128]{0,1:T(8,128)}), f32[4096,128]{0,1:T(8,128)}) %all-gather.5.cloned.1.call-update) | async-done | bytes 2097168 | tf_op jit(solution)/shard_map/while/body/eval_jaxpr/all_gather | solution.py:31
  1331.4 59.2 %all-gather.3.cloned.1.call-done = f32[4096,128]{0,1:T(8,128)} async-done(((f32[512,128]{0,1:T(8,128)}), f32[4096,128]{0,1:T(8,128)}) %all-gather.3.cloned.1.call-update) | async-done | bytes 2097168 | tf_op jit(solution)/shard_map/while/body/eval_jaxpr/all_gather | solution.py:31
  1392.4 4.5 fusion.65
  1396.9 53.7 %all-gather.5.cloned.1.call-done = f32[4096,128]{0,1:T(8,128)} async-done(((f32[512,128]{0,1:T(8,128)}), f32[4096,128]{0,1:T(8,128)}) %all-gather.5.cloned.1.call-update) | async-done | bytes 2097168 | tf_op jit(solution)/shard_map/while/body/eval_jaxpr/all_gather | solution.py:31
  1462.8 59.2 %all-gather.3.cloned.1.call-done = f32[4096,128]{0,1:T(8,128)} async-done(((f32[512,128]{0,1:T(8,128)}), f32[4096,128]{0,1:T(8,128)}) %all-gather.3.cloned.1.call-update) | async-done | bytes 2097168 | tf_op jit(solution)/shard_map/while/body/eval_jaxpr/all_gather | solution.py:31
  1523.8 4.5 fusion.65
  1528.3 53.7 %all-gather.5.cloned.1.call-done = f32[4096,128]{0,1:T(8,128)} async-done(((f32[512,128]{0,1:T(8,128)}), f32[4096,128]{0,1:T(8,128)}) %all-gather.5.cloned.1.call-update) | async-done | bytes 2097168 | tf_op jit(solution)/shard_map/while/body/eval_jaxpr/all_gather | solution.py:31
  1594.2 59.2 %all-gather.3.cloned.1.call-done = f32[4096,128]{0,1:T(8,128)} async-done(((f32[512,128]{0,1:T(8,128)}), f32[4096,128]{0,1:T(8,128)}) %all-gather.3.cloned.1.call-update) | async-done | bytes 2097168 | tf_op jit(solution)/shard_map/while/body/eval_jaxpr/all_gather | solution.py:31
  1655.2 4.5 fusion.65
  1659.7 53.7 %all-gather.5.cloned.1.call-done = f32[4096,128]{0,1:T(8,128)} async-done(((f32[512,128]{0,1:T(8,128)}), f32[4096,128]{0,1:T(8,128)}) %all-gather.5.cloned.1.call-update) | async-done | bytes 2097168 | tf_op jit(solution)/shard_map/while/body/eval_jaxpr/all_gather | solution.py:31
  1725.6 58.8 %all-gather.3.cloned.1.call-done = f32[4096,128]{0,1:T(8,128)} async-done(((f32[512,128]{0,1:T(8,128)}), f32[4096,128]{0,1:T(8,128)}) %all-gather.3.cloned.1.call-update) | async-done | bytes 2097168 | tf_op jit(solution)/shard_map/while/body/eval_jaxpr/all_gather | solution.py:31
  1786.3 4.5 fusion.65
  1790.8 53.6 %all-gather.5.cloned.1.call-done = f32[4096,128]{0,1:T(8,128)} async-done(((f32[512,128]{0,1:T(8,128)}), f32[4096,128]{0,1:T(8,128)}) %all-gather.5.cloned.1.call-update) | async-done | bytes 2097168 | tf_op jit(solution)/shard_map/while/body/eval_jaxpr/all_gather | solution.py:31
  1856.7 59.2 %all-gather.3.cloned.1.call-done = f32[4096,128]{0,1:T(8,128)} async-done(((f32[512,128]{0,1:T(8,128)}), f32[4096,128]{0,1:T(8,128)}) %all-gather.3.cloned.1.call-update) | async-done | bytes 2097168 | tf_op jit(solution)/shard_map/while/body/eval_jaxpr/all_gather | solution.py:31
  1917.7 4.5 fusion.65
  1922.2 53.7 %all-gather.5.cloned.1.call-done = f32[4096,128]{0,1:T(8,128)} async-done(((f32[512,128]{0,1:T(8,128)}), f32[4096,128]{0,1:T(8,128)}) %all-gather.5.cloned.1.call-update) | async-done | bytes 2097168 | tf_op jit(solution)/shard_map/while/body/eval_jaxpr/all_gather | solution.py:31
  1988.1 59.2 %all-gather.3.cloned.1.call-done = f32[4096,128]{0,1:T(8,128)} async-done(((f32[512,128]{0,1:T(8,128)}), f32[4096,128]{0,1:T(8,128)}) %all-gather.3.cloned.1.call-update) | async-done | bytes 2097168 | tf_op jit(solution)/shard_map/while/body/eval_jaxpr/all_gather | solution.py:31
  2049.1 4.5 fusion.65
  2053.6 53.7 %all-gather.5.cloned.1.call-done = f32[4096,128]{0,1:T(8,128)} async-done(((f32[512,128]{0,1:T(8,128)}), f32[4096,128]{0,1:T(8,128)}) %all-gather.5.cloned.1.call-update) | async-done | bytes 2097168 | tf_op jit(solution)/shard_map/while/body/eval_jaxpr/all_gather | solution.py:31
  (499 shorter events, 254.1 us)
Async XLA Ops:
  16.4 61.1 %all-gather.3.cloned.1.call-start = ((), (), s32[]{:S(2)}) async-start(), calls=%async_computation | async-start | bytes 2359296 | tf_op jit(solution)/shard_map/while/body/eval_jaxpr/all_gather | solution.py:31
  17.1 120.4 %all-gather.5.cloned.1.call-start = ((), (), s32[]{:S(2)}) async-start(), calls=%async_computation.1 | async-start | bytes 2359296 | tf_op jit(solution)/shard_map/while/body/eval_jaxpr/all_gather | solution.py:31
  143.4 2.9 collective-permute-start
  148.1 60.8 %all-gather.3.cloned.1.call-start = ((), (), s32[]{:S(2)}) async-start(), calls=%async_computation | async-start | bytes 2359296 | tf_op jit(solution)/shard_map/while/body/eval_jaxpr/all_gather | solution.py:31
  148.8 120.1 %all-gather.5.cloned.1.call-start = ((), (), s32[]{:S(2)}) async-start(), calls=%async_computation.1 | async-start | bytes 2359296 | tf_op jit(solution)/shard_map/while/body/eval_jaxpr/all_gather | solution.py:31
  274.8 2.9 collective-permute-start
  279.5 60.5 %all-gather.3.cloned.1.call-start = ((), (), s32[]{:S(2)}) async-start(), calls=%async_computation | async-start | bytes 2359296 | tf_op jit(solution)/shard_map/while/body/eval_jaxpr/all_gather | solution.py:31
  280.2 119.8 %all-gather.5.cloned.1.call-start = ((), (), s32[]{:S(2)}) async-start(), calls=%async_computation.1 | async-start | bytes 2359296 | tf_op jit(solution)/shard_map/while/body/eval_jaxpr/all_gather | solution.py:31
  405.9 2.9 collective-permute-start
  410.6 60.8 %all-gather.3.cloned.1.call-start = ((), (), s32[]{:S(2)}) async-start(), calls=%async_computation | async-start | bytes 2359296 | tf_op jit(solution)/shard_map/while/body/eval_jaxpr/all_gather | solution.py:31
  411.3 120.1 %all-gather.5.cloned.1.call-start = ((), (), s32[]{:S(2)}) async-start(), calls=%async_computation.1 | async-start | bytes 2359296 | tf_op jit(solution)/shard_map/while/body/eval_jaxpr/all_gather | solution.py:31
  537.3 2.9 collective-permute-start
  542.0 60.8 %all-gather.3.cloned.1.call-start = ((), (), s32[]{:S(2)}) async-start(), calls=%async_computation | async-start | bytes 2359296 | tf_op jit(solution)/shard_map/while/body/eval_jaxpr/all_gather | solution.py:31
  542.7 120.1 %all-gather.5.cloned.1.call-start = ((), (), s32[]{:S(2)}) async-start(), calls=%async_computation.1 | async-start | bytes 2359296 | tf_op jit(solution)/shard_map/while/body/eval_jaxpr/all_gather | solution.py:31
  668.7 2.9 collective-permute-start
  673.4 60.8 %all-gather.3.cloned.1.call-start = ((), (), s32[]{:S(2)}) async-start(), calls=%async_computation | async-start | bytes 2359296 | tf_op jit(solution)/shard_map/while/body/eval_jaxpr/all_gather | solution.py:31
  674.1 120.1 %all-gather.5.cloned.1.call-start = ((), (), s32[]{:S(2)}) async-start(), calls=%async_computation.1 | async-start | bytes 2359296 | tf_op jit(solution)/shard_map/while/body/eval_jaxpr/all_gather | solution.py:31
  800.1 2.9 collective-permute-start
  804.7 60.8 %all-gather.3.cloned.1.call-start = ((), (), s32[]{:S(2)}) async-start(), calls=%async_computation | async-start | bytes 2359296 | tf_op jit(solution)/shard_map/while/body/eval_jaxpr/all_gather | solution.py:31
  805.5 120.1 %all-gather.5.cloned.1.call-start = ((), (), s32[]{:S(2)}) async-start(), calls=%async_computation.1 | async-start | bytes 2359296 | tf_op jit(solution)/shard_map/while/body/eval_jaxpr/all_gather | solution.py:31
  931.5 2.9 collective-permute-start
  936.2 60.5 %all-gather.3.cloned.1.call-start = ((), (), s32[]{:S(2)}) async-start(), calls=%async_computation | async-start | bytes 2359296 | tf_op jit(solution)/shard_map/while/body/eval_jaxpr/all_gather | solution.py:31
  936.9 119.8 %all-gather.5.cloned.1.call-start = ((), (), s32[]{:S(2)}) async-start(), calls=%async_computation.1 | async-start | bytes 2359296 | tf_op jit(solution)/shard_map/while/body/eval_jaxpr/all_gather | solution.py:31
  1062.6 2.9 collective-permute-start
  1067.2 60.5 %all-gather.3.cloned.1.call-start = ((), (), s32[]{:S(2)}) async-start(), calls=%async_computation | async-start | bytes 2359296 | tf_op jit(solution)/shard_map/while/body/eval_jaxpr/all_gather | solution.py:31
  1068.0 119.8 %all-gather.5.cloned.1.call-start = ((), (), s32[]{:S(2)}) async-start(), calls=%async_computation.1 | async-start | bytes 2359296 | tf_op jit(solution)/shard_map/while/body/eval_jaxpr/all_gather | solution.py:31
  1193.7 2.9 collective-permute-start
  1198.3 60.8 %all-gather.3.cloned.1.call-start = ((), (), s32[]{:S(2)}) async-start(), calls=%async_computation | async-start | bytes 2359296 | tf_op jit(solution)/shard_map/while/body/eval_jaxpr/all_gather | solution.py:31
  1199.1 120.1 %all-gather.5.cloned.1.call-start = ((), (), s32[]{:S(2)}) async-start(), calls=%async_computation.1 | async-start | bytes 2359296 | tf_op jit(solution)/shard_map/while/body/eval_jaxpr/all_gather | solution.py:31
  1325.1 2.9 collective-permute-start
  1329.7 60.8 %all-gather.3.cloned.1.call-start = ((), (), s32[]{:S(2)}) async-start(), calls=%async_computation | async-start | bytes 2359296 | tf_op jit(solution)/shard_map/while/body/eval_jaxpr/all_gather | solution.py:31
  1330.5 120.1 %all-gather.5.cloned.1.call-start = ((), (), s32[]{:S(2)}) async-start(), calls=%async_computation.1 | async-start | bytes 2359296 | tf_op jit(solution)/shard_map/while/body/eval_jaxpr/all_gather | solution.py:31
  1456.5 2.9 collective-permute-start
  1461.1 60.8 %all-gather.3.cloned.1.call-start = ((), (), s32[]{:S(2)}) async-start(), calls=%async_computation | async-start | bytes 2359296 | tf_op jit(solution)/shard_map/while/body/eval_jaxpr/all_gather | solution.py:31
  1461.9 120.1 %all-gather.5.cloned.1.call-start = ((), (), s32[]{:S(2)}) async-start(), calls=%async_computation.1 | async-start | bytes 2359296 | tf_op jit(solution)/shard_map/while/body/eval_jaxpr/all_gather | solution.py:31
  1587.9 2.9 collective-permute-start
  1592.5 60.8 %all-gather.3.cloned.1.call-start = ((), (), s32[]{:S(2)}) async-start(), calls=%async_computation | async-start | bytes 2359296 | tf_op jit(solution)/shard_map/while/body/eval_jaxpr/all_gather | solution.py:31
  1593.3 120.1 %all-gather.5.cloned.1.call-start = ((), (), s32[]{:S(2)}) async-start(), calls=%async_computation.1 | async-start | bytes 2359296 | tf_op jit(solution)/shard_map/while/body/eval_jaxpr/all_gather | solution.py:31
  1719.3 2.9 collective-permute-start
  1723.9 60.5 %all-gather.3.cloned.1.call-start = ((), (), s32[]{:S(2)}) async-start(), calls=%async_computation | async-start | bytes 2359296 | tf_op jit(solution)/shard_map/while/body/eval_jaxpr/all_gather | solution.py:31
  1724.7 119.8 %all-gather.5.cloned.1.call-start = ((), (), s32[]{:S(2)}) async-start(), calls=%async_computation.1 | async-start | bytes 2359296 | tf_op jit(solution)/shard_map/while/body/eval_jaxpr/all_gather | solution.py:31
  1850.4 2.9 collective-permute-start
  1855.0 60.8 %all-gather.3.cloned.1.call-start = ((), (), s32[]{:S(2)}) async-start(), calls=%async_computation | async-start | bytes 2359296 | tf_op jit(solution)/shard_map/while/body/eval_jaxpr/all_gather | solution.py:31
  1855.8 120.1 %all-gather.5.cloned.1.call-start = ((), (), s32[]{:S(2)}) async-start(), calls=%async_computation.1 | async-start | bytes 2359296 | tf_op jit(solution)/shard_map/while/body/eval_jaxpr/all_gather | solution.py:31
  1981.7 2.9 collective-permute-start
  1986.4 60.8 %all-gather.3.cloned.1.call-start = ((), (), s32[]{:S(2)}) async-start(), calls=%async_computation | async-start | bytes 2359296 | tf_op jit(solution)/shard_map/while/body/eval_jaxpr/all_gather | solution.py:31
  1987.1 120.1 %all-gather.5.cloned.1.call-start = ((), (), s32[]{:S(2)}) async-start(), calls=%async_computation.1 | async-start | bytes 2359296 | tf_op jit(solution)/shard_map/while/body/eval_jaxpr/all_gather | solution.py:31
  2113.1 2.9 collective-permute-start
  (115 other events, 381.9 us)
Sparse Core Ops, SparseCore 0:
  20.1 57.3 all-gather.2
  83.9 53.5 all-gather.4
  151.8 57.0 all-gather.2
  215.3 53.5 all-gather.4
  282.9 57.0 all-gather.2
  346.4 53.5 all-gather.4
  414.3 57.0 all-gather.2
  477.8 53.5 all-gather.4
  545.7 57.0 all-gather.2
  609.2 53.5 all-gather.4
  677.1 57.0 all-gather.2
  740.6 53.5 all-gather.4
  808.5 57.0 all-gather.2
  872.0 53.5 all-gather.4
  939.6 57.0 all-gather.2
  1003.1 53.5 all-gather.4
  1070.7 57.0 all-gather.2
  1134.2 53.5 all-gather.4
  1202.1 57.0 all-gather.2
  1265.6 53.5 all-gather.4
  1333.5 57.0 all-gather.2
  1397.0 53.5 all-gather.4
  1464.9 57.0 all-gather.2
  1528.4 53.5 all-gather.4
  1596.3 57.0 all-gather.2
  1659.8 53.5 all-gather.4
  1727.4 57.0 all-gather.2
  1790.9 53.5 all-gather.4
  1858.8 57.0 all-gather.2
  1922.3 53.5 all-gather.4
  1990.2 57.0 all-gather.2
  2053.7 53.5 all-gather.4
where the time goes:
time: 2150 us; the launch traced here: 2140 us
  waiting for transfers between devices  1800 us (84%)
  matrix products  139 us (6%)
  other arithmetic  112 us (5%)
  local copies, waits for them, and re-layouts  48.1 us (2%)
  starting transfers between devices  21.6 us (1%)
    all_gather x32, waiting for transfers between devices, advance(): full = lax.all_gather(current, 'tile', axis=0, tiled=True)  1800 us
    dot_general x32, matrix products, advance(): jnp.dot(interface[layer_num], phased, preferred_element_type=jnp.float32)  134 us
    another operation x32, other arithmetic  59.8 us
  transfers between devices with their start and end apart: 48, of which 32 were waited for; matrix products, arithmetic and copies ran while one was open for 2% of the time, Pallas kernels for 0%

commit v1 on v0

v1 whole, which is shorter than its diff:
```python
import functools

import jax
import jax.numpy as jnp
from jax import lax
from jax.experimental import pallas as pl
from jax.experimental.pallas import tpu as pltpu
from jax.sharding import PartitionSpec as P

DEPTHS = 4
CHUNKS = 4
NT = (((1,), (1,)), ((), ()))


def step_kernel(full_ref, cos_ref, sin_ref, mat_ref, out_ref, mat_buf, sems, *, layer):
    blocks, wide, rows = full_ref.shape
    half = wide // 2
    copies = [
        pltpu.make_async_copy(
            mat_ref.at[layer, :, pl.ds(b * rows, rows)], mat_buf.at[b], sems.at[b]
        )
        for b in range(blocks)
    ]
    for copy in copies:
        copy.start()
    total = jnp.zeros((wide, rows), jnp.float32)
    for b in range(blocks):
        cosine = cos_ref[b : b + 1, :]
        sine = sin_ref[b : b + 1, :]
        real_part = full_ref[b, :half, :]
        imag_part = full_ref[b, half:, :]
        phased = jnp.concatenate(
            [cosine * real_part - sine * imag_part, sine * real_part + cosine * imag_part], axis=0
        ).astype(jnp.bfloat16)
        copies[b].wait()
        total += lax.dot_general(phased, mat_buf[b], NT, preferred_element_type=jnp.float32)
    for b in range(blocks):
        out_ref[b] = total


def layer_step(full, cosine, sine, mats, layer):
    blocks, wide, rows = full.shape
    vmem = pl.BlockSpec(memory_space=pltpu.VMEM)
    return pl.pallas_call(
        functools.partial(step_kernel, layer=layer),
        out_shape=jax.ShapeDtypeStruct(full.shape, jnp.float32),
        in_specs=[vmem, vmem, vmem, pl.BlockSpec(memory_space=pl.ANY)],
        out_specs=vmem,
        scratch_shapes=[
            pltpu.VMEM((blocks, rows, rows), jnp.bfloat16),
            pltpu.SemaphoreType.DMA((blocks,)),
        ],
        compiler_params=pltpu.CompilerParams(vmem_limit_bytes=24 * 1024 * 1024),
    )(full, cosine, sine, mats)


def fields_kernel(enter_ref, cos_ref, sin_ref, mat_ref, out_ref, total):
    step = pl.program_id(1)
    chunks, _, wide, rows = enter_ref.shape[1:]
    half = wide // 2
    real_part = enter_ref[0, :, 0, :half, :].reshape(chunks * half, rows)
    imag_part = enter_ref[0, :, 0, half:, :].reshape(chunks * half, rows)
    parts = [real_part.astype(jnp.bfloat16), imag_part.astype(jnp.bfloat16)]
    for depth in range(1, DEPTHS):
        cosine = cos_ref[0, 0, depth - 1 : depth, :]
        sine = sin_ref[0, 0, depth - 1 : depth, :]
        parts.append((cosine * real_part - sine * imag_part).astype(jnp.bfloat16))
        parts.append((sine * real_part + cosine * imag_part).astype(jnp.bfloat16))
    depths = jnp.concatenate(parts, axis=0)
    partial = lax.dot_general(mat_ref[0], depths, NT, preferred_element_type=jnp.float32)

    @pl.when(step == 0)
    def _():
        total[...] = partial

    @pl.when(step > 0)
    def _():
        total[...] += partial

    @pl.when(step == pl.num_programs(1) - 1)
    def _():
        out_ref[0] = total[...].astype(jnp.bfloat16)


def all_fields(enters, cosines, sines, eigvec):
    layers, chunks, blocks, wide, rows = enters.shape
    orders = eigvec.shape[2]
    cols = DEPTHS * chunks * wide
    coef = pl.BlockSpec((1, 1, DEPTHS - 1, rows), lambda i, b: (i, b, 0, 0))
    return pl.pallas_call(
        fields_kernel,
        out_shape=jax.ShapeDtypeStruct((layers, rows, cols), jnp.bfloat16),
        grid=(layers, blocks),
        in_specs=[
            pl.BlockSpec((1, chunks, 1, wide, rows), lambda i, b: (i, 0, b, 0, 0)),
            coef,
            coef,
            pl.BlockSpec((1, rows, rows), lambda i, b: (i, 0, b)),
        ],
        out_specs=pl.BlockSpec((1, rows, cols), lambda i, b: (i, 0, 0)),
        scratch_shapes=[pltpu.VMEM((rows, cols), jnp.float32)],
        compiler_params=pltpu.CompilerParams(vmem_limit_bytes=32 * 1024 * 1024),
    )(enters, cosines, sines, eigvec)


def to_all(block):
    return lax.all_to_all(block, "tile", split_axis=0, concat_axis=0, tiled=False)


def on_device(incident, interface, eigvec, angle, decay):
    groups = lax.axis_size("layer")
    tiles = lax.axis_size("tile")
    member = lax.axis_index("layer")
    layers, rows, orders = interface.shape
    width = incident.shape[1]
    half = width // 2
    part = half // CHUNKS
    wide = 2 * part

    angle = angle.reshape(layers, tiles, 1, rows)
    decay = decay.reshape(layers, tiles, 1, rows)
    fracs = (jnp.arange(1, DEPTHS + 1, dtype=jnp.float32) / DEPTHS).reshape(1, 1, DEPTHS, 1)
    scale = jnp.exp(-fracs * decay)
    cosines = scale * jnp.cos(fracs * angle)
    sines = scale * jnp.sin(fracs * angle)
    whole_cos, whole_sin = cosines[:, :, DEPTHS - 1], sines[:, :, DEPTHS - 1]

    start = incident.astype(jnp.float32).T.reshape(2, CHUNKS, part, rows)
    start = start.transpose(1, 0, 2, 3).reshape(CHUNKS, wide, rows)

    ring = [(i, (i + 1) % groups) for i in range(groups)]
    enters = jnp.zeros((layers, CHUNKS + 1, tiles, wide, rows), jnp.float32)
    leaves = jnp.zeros((layers, CHUNKS + 1, wide, rows), jnp.float32)
    received = None
    for tick in range(groups + CHUNKS - 1):
        own = start[min(tick, CHUNKS - 1)]
        inbox = own if received is None else jnp.where(member == 0, own, received)
        slot = jnp.clip(tick - member, 0, CHUNKS)
        spread = jnp.broadcast_to(inbox[None], (tiles, wide, rows))
        for layer in range(layers):
            full = to_all(spread)
            spread = layer_step(full, whole_cos[layer], whole_sin[layer], interface, layer)
            enters = lax.dynamic_update_slice(enters, full[None, None], (layer, slot, 0, 0, 0))
            leaves = lax.dynamic_update_slice(leaves, spread[:1][None], (layer, slot, 0, 0))
        received = lax.ppermute(spread[0], "layer", ring)

    fields = all_fields(
        enters[:, :CHUNKS], cosines[:, :, : DEPTHS - 1], sines[:, :, : DEPTHS - 1], eigvec
    )
    leaving = leaves[:, :CHUNKS].reshape(layers, CHUNKS, 2, part, rows)
    leaving = leaving.transpose(0, 4, 2, 1, 3).reshape(layers, rows, width)
    return fields, leaving


def solution(mesh):
    in_specs = (
        P("tile", None),
        P("layer", "tile", None),
        P("layer", "tile", None),
        P("layer", None),
        P("layer", None),
    )
    out_specs = (P("layer", "tile", None), P("layer", "tile", None))
    return jax.shard_map(
        on_device, mesh=mesh, in_specs=in_specs, out_specs=out_specs, check_vma=False
    )
```

time: 2150 us -> 882 us (0.41)
  waiting for transfers between devices: 1800 us -> 307 us
  local copies, waits for them, and re-layouts: 48.1 us -> 241 us
  matrix products: 139 us -> 0 us
  other arithmetic: 112 us -> 0.74 us
  Pallas kernels: 0 us -> 109 us
  starting transfers between devices: 21.6 us -> 117 us
  blocking collectives: 0 us -> 90.6 us
    all_gather x32 -> x0, waiting for transfers between devices: 1800 us -> none  [advance(): full = lax.all_gather(current, 'tile', axis=0, tiled=True)]
    all_to_all x0 -> x31, waiting for transfers between devices: none -> 223 us  [to_all(): lax.all_to_all(block, 'tile', split_axis=0, concat_axis=0, tiled=False)]
    dot_general x34 -> x0, matrix products: 139 us -> none  [the longest x32 134 us: advance(): jnp.dot(interface[layer_num], phased, preferred_element_type=jnp.float32)]
    unnamed x9 -> x126, local copies, waits for them, and re-layouts: 6.16 us -> 125 us
    all_to_all x0 -> x31, starting transfers between devices: none -> 116 us  [to_all(): lax.all_to_all(block, 'tile', split_axis=0, concat_axis=0, tiled=False)]
    pallas_call x0 -> x39, Pallas kernels: none -> 109 us  [the longest x38 97.3 us: layer_step(): pl.pallas_call(functools.partial(step_kernel, layer=layer), out_shape=jax...]
    all_to_all x0 -> x7, blocking collectives: none -> 90.6 us  [to_all(): lax.all_to_all(block, 'tile', split_axis=0, concat_axis=0, tiled=False)]
    dynamic_update_slice x0 -> x76, local copies, waits for them, and re-layouts: none -> 88.8 us  [the longest x38 52.2 us: on_device(): lax.dynamic_update_slice(leaves, spread[:1][None], (layer, slot, 0, 0))]
  transfers between devices with their start and end apart: 48 -> 49, of which waited for: 32 -> 49; matrix products, arithmetic and copies ran while one was open for 2% -> 11% of each run, Pallas kernels for 0% -> 0%
where the time goes in v1:
time: 882 us; the launch traced here: 868 us
  waiting for transfers between devices  307 us (35%)
  local copies, waits for them, and re-layouts  241 us (27%)
  starting transfers between devices  117 us (13%)
  Pallas kernels  109 us (12%)
  blocking collectives  90.6 us (10%)
    all_to_all x31, waiting for transfers between devices, to_all(): lax.all_to_all(block, 'tile', split_axis=0, concat_axis=0, tiled=False)  223 us
    unnamed x126, local copies, waits for them, and re-layouts  125 us
    all_to_all x31, starting transfers between devices, to_all(): lax.all_to_all(block, 'tile', split_axis=0, concat_axis=0, tiled=False)  116 us
    pallas_call x38, Pallas kernels, layer_step(): pl.pallas_call(functools.partial(step_kernel, layer=layer), out_shape=jax...  97.3 us
    all_to_all x7, blocking collectives, to_all(): lax.all_to_all(block, 'tile', split_axis=0, concat_axis=0, tiled=False)  90.6 us
    ppermute x18, waiting for transfers between devices, on_device(): received = lax.ppermute(spread[0], 'layer', ring)  83.6 us
    dynamic_update_slice x38, local copies, waits for them, and re-layouts, on_device(): lax.dynamic_update_slice(leaves, spread[:1][None], (layer, slot, 0, 0))  52.2 us
    dynamic_update_slice x38, local copies, waits for them, and re-layouts, on_device(): lax.dynamic_update_slice(enters, full[None, None], (layer, slot, 0, 0, 0))  36.6 us
  transfers between devices with their start and end apart: 49, of which 49 were waited for; matrix products, arithmetic and copies ran while one was open for 11% of the time, Pallas kernels for 0%

profile of v1, /device:TPU:0, one launch (start us, length us, event | category | flops | bytes accessed | tf_op | source)
XLA Modules:
  0.0 867.9 jit_solution(13081762694809997131)
XLA Ops:
  2.6 7.7 all-to-all-start
  12.4 8.8 %all-to-all-done.full_ref = f32[8,32,512]{2,1,0:T(8,128)S(1)} async-done(((f32[8,32,512]{2,1,0:T(8,128)}), f32[8,32,512]{2,1,0:T(8,128)S(1)}, u32[]{:S(2)}, u32[]{:S(2)}) %all-to-all-start) | async-done | bytes 524320 | tf_op jit(solution)/shard_map/all_to_all | solution.py:107
  26.7 14.2 %all_to_all.190.full_ref = f32[8,32,512]{2,1,0:T(8,128)S(1)} all-to-all(f32[8,32,512]{2,1,0:T(8,128)S(1)} %shard_map.68), channel_id=1, replica_groups=mesh['layer'=16,'tile'=8] {'tile'}, dimensions={0} | all-to-all | bytes 1048576 | tf_op jit(solution)/shard_map/all_to_all | solution.py:107
  44.0 5.8 collective-permute-done
  49.8 12.7 %all_to_all.191.full_ref = f32[8,32,512]{2,1,0:T(8,128)S(1)} all-to-all(f32[8,32,512]{2,1,0:T(8,128)S(1)} %broadcast_in_dim.354), channel_id=1, replica_groups=mesh['layer'=16,'tile'=8] {'tile'}, dimensions={0} | all-to-all | bytes 1048576 | tf_op jit(solution)/shard_map/all_to_all | solution.py:107
  68.2 12.9 %all_to_all.192.full_ref = f32[8,32,512]{2,1,0:T(8,128)S(1)} all-to-all(f32[8,32,512]{2,1,0:T(8,128)S(1)} %shard_map.70), channel_id=1, replica_groups=mesh['layer'=16,'tile'=8] {'tile'}, dimensions={0} | all-to-all | bytes 1048576 | tf_op jit(solution)/shard_map/all_to_all | solution.py:107
  83.4 5.8 collective-permute-done.1
  89.2 12.7 %all_to_all.193.full_ref = f32[8,32,512]{2,1,0:T(8,128)S(1)} all-to-all(f32[8,32,512]{2,1,0:T(8,128)S(1)} %broadcast_in_dim.357), channel_id=1, replica_groups=mesh['layer'=16,'tile'=8] {'tile'}, dimensions={0} | all-to-all | bytes 1048576 | tf_op jit(solution)/shard_map/all_to_all | solution.py:107
  105.0 12.7 %all_to_all.194.full_ref = f32[8,32,512]{2,1,0:T(8,128)S(1)} all-to-all(f32[8,32,512]{2,1,0:T(8,128)S(1)} %shard_map.72), channel_id=1, replica_groups=mesh['layer'=16,'tile'=8] {'tile'}, dimensions={0} | all-to-all | bytes 1048576 | tf_op jit(solution)/shard_map/all_to_all | solution.py:107
  120.0 5.8 collective-permute-done.2
  125.9 12.7 %all_to_all.195.full_ref = f32[8,32,512]{2,1,0:T(8,128)S(1)} all-to-all(f32[8,32,512]{2,1,0:T(8,128)S(1)} %broadcast_in_dim.360), channel_id=1, replica_groups=mesh['layer'=16,'tile'=8] {'tile'}, dimensions={0} | all-to-all | bytes 1048576 | tf_op jit(solution)/shard_map/all_to_all | solution.py:107
  141.6 12.7 %all_to_all.196.full_ref = f32[8,32,512]{2,1,0:T(8,128)S(1)} all-to-all(f32[8,32,512]{2,1,0:T(8,128)S(1)} %shard_map.74), channel_id=1, replica_groups=mesh['layer'=16,'tile'=8] {'tile'}, dimensions={0} | all-to-all | bytes 1048576 | tf_op jit(solution)/shard_map/all_to_all | solution.py:107
  193.2 7.3 all-to-all-done.9.full_ref
  220.9 7.3 all-to-all-done.10.full_ref
  240.5 7.3 all-to-all-done.11.full_ref
  266.6 7.3 all-to-all-done.12.full_ref
  286.1 7.3 all-to-all-done.13.full_ref
  300.0 4.9 collective-permute-done.6
  312.6 6.2 all-to-all-done.14.full_ref
  332.3 6.2 all-to-all-done.15.full_ref
  358.1 7.3 all-to-all-done.16.full_ref
  378.7 7.3 all-to-all-done.17.full_ref
  392.6 4.9 collective-permute-done.8
  404.2 7.3 all-to-all-done.18.full_ref
  423.7 7.3 all-to-all-done.19.full_ref
  449.1 7.3 all-to-all-done.20.full_ref
  469.7 6.2 all-to-all-done.21.full_ref
  482.5 4.9 collective-permute-done.10
  494.1 7.3 all-to-all-done.22.full_ref
  513.8 7.3 all-to-all-done.23.full_ref
  539.3 7.3 all-to-all-done.24.full_ref
  558.8 7.3 all-to-all-done.25.full_ref
  584.3 7.3 all-to-all-done.26.full_ref
  603.8 7.3 all-to-all-done.27.full_ref
  629.2 7.3 all-to-all-done.28.full_ref
  648.7 7.3 all-to-all-done.29.full_ref
  662.5 4.9 collective-permute-done.14
  673.3 8.1 all-to-all-done.30.full_ref
  693.9 7.3 all-to-all-done.31.full_ref
  719.3 7.3 all-to-all-done.32.full_ref
  738.0 8.1 all-to-all-done.33.full_ref
  752.6 4.9 collective-permute-done.16
  764.3 7.3 all-to-all-done.34.full_ref
  782.9 8.1 all-to-all-done.35.full_ref
  808.4 8.1 all-to-all-done.36.full_ref
  828.7 7.3 all-to-all-done.37.full_ref
  836.8 5.1 slice.345.enter_ref
  855.8 11.7 %shard_map.105 = bf16[2,512,512]{2,1,0:T(8,128)(2,1)} custom-call(f32[2,4,8,32,512]{4,3,2,1,0:T(8,128)S(1)} %copy-done.34, f32[2,8,3,512]{3,2,1,0:T(4,128)S(1)} %copy.11.cos_ref, f32[2,8,3,512]{3,2,1,0:T(4,128)S(1)} %copy.12.sin_ref, bf16[2,512,4096]{2,1,0:T(8,128)(2,1)S(1)} %copy-done.35), custom_call_target="tpu_custom_call" | custom-call | tf_op jit(solution)/shard_map/pallas_call | solution.py:90
  (368 shorter events, 488.8 us)
Async XLA Ops:
  2.6 18.6 %all-to-all-start = ((f32[8,32,512]{2,1,0:T(8,128)}), f32[8,32,512]{2,1,0:T(8,128)S(1)}, u32[]{:S(2)}, u32[]{:S(2)}) async-start(f32[8,32,512]{2,1,0:T(8,128)} %broadcast_in_dim.351), calls=%async_computation | async-start | bytes 1048576 | tf_op jit(solution)/shard_map/all_to_all | solution.py:107
  44.0 5.8 collective-permute-start
  83.3 5.9 collective-permute-start.1
  119.9 5.9 collective-permute-start.2
  158.0 6.6 collective-permute-start.3
  165.4 13.8 %all-to-all-start.8 = ((f32[8,32,512]{2,1,0:T(8,128)}), f32[8,32,512]{2,1,0:T(8,128)}, u32[]{:S(2)}, u32[]{:S(2)}) async-start(f32[8,32,512]{2,1,0:T(8,128)} %broadcast_in_dim.363), calls=%async_computation.8 | async-start | bytes 1048576 | tf_op jit(solution)/shard_map/all_to_all | solution.py:107
  186.7 13.8 %all-to-all-start.9 = ((f32[8,32,512]{2,1,0:T(8,128)}), f32[8,32,512]{2,1,0:T(8,128)}, u32[]{:S(2)}, u32[]{:S(2)}) async-start(f32[8,32,512]{2,1,0:T(8,128)} %copy-done.45), calls=%async_computation.9 | async-start | bytes 1048576 | tf_op jit(solution)/shard_map/all_to_all | solution.py:107
  208.0 5.8 collective-permute-start.4
  214.7 13.5 %all-to-all-start.10 = ((f32[8,32,512]{2,1,0:T(8,128)}), f32[8,32,512]{2,1,0:T(8,128)S(1)}, u32[]{:S(2)}, u32[]{:S(2)}) async-start(f32[8,32,512]{2,1,0:T(8,128)} %broadcast_in_dim.366), calls=%async_computation.10 | async-start | bytes 1048576 | tf_op jit(solution)/shard_map/all_to_all | solution.py:107
  234.6 13.1 %all-to-all-start.11 = ((f32[8,32,512]{2,1,0:T(8,128)}), f32[8,32,512]{2,1,0:T(8,128)S(1)}, u32[]{:S(2)}, u32[]{:S(2)}) async-start(f32[8,32,512]{2,1,0:T(8,128)} %shard_map.78), calls=%async_computation.11 | async-start | bytes 1048576 | tf_op jit(solution)/shard_map/all_to_all | solution.py:107
  254.1 5.8 collective-permute-start.5
  260.8 13.1 %all-to-all-start.12 = ((f32[8,32,512]{2,1,0:T(8,128)}), f32[8,32,512]{2,1,0:T(8,128)S(1)}, u32[]{:S(2)}, u32[]{:S(2)}) async-start(f32[8,32,512]{2,1,0:T(8,128)} %broadcast_in_dim.369), calls=%async_computation.12 | async-start | bytes 1048576 | tf_op jit(solution)/shard_map/all_to_all | solution.py:107
  280.3 13.1 %all-to-all-start.13 = ((f32[8,32,512]{2,1,0:T(8,128)}), f32[8,32,512]{2,1,0:T(8,128)S(1)}, u32[]{:S(2)}, u32[]{:S(2)}) async-start(f32[8,32,512]{2,1,0:T(8,128)} %shard_map.80), calls=%async_computation.13 | async-start | bytes 1048576 | tf_op jit(solution)/shard_map/all_to_all | solution.py:107
  299.0 5.9 collective-permute-start.6
  305.7 13.1 %all-to-all-start.14 = ((f32[8,32,512]{2,1,0:T(8,128)}), f32[8,32,512]{2,1,0:T(8,128)S(1)}, u32[]{:S(2)}, u32[]{:S(2)}) async-start(f32[8,32,512]{2,1,0:T(8,128)} %broadcast_in_dim.372), calls=%async_computation.14 | async-start | bytes 1048576 | tf_op jit(solution)/shard_map/all_to_all | solution.py:107
  325.2 13.3 %all-to-all-start.15 = ((f32[8,32,512]{2,1,0:T(8,128)}), f32[8,32,512]{2,1,0:T(8,128)S(1)}, u32[]{:S(2)}, u32[]{:S(2)}) async-start(f32[8,32,512]{2,1,0:T(8,128)} %shard_map.82), calls=%async_computation.15 | async-start | bytes 1048576 | tf_op jit(solution)/shard_map/all_to_all | solution.py:107
  351.6 13.8 %all-to-all-start.16 = ((f32[8,32,512]{2,1,0:T(8,128)}), f32[8,32,512]{2,1,0:T(8,128)}, u32[]{:S(2)}, u32[]{:S(2)}) async-start(f32[8,32,512]{2,1,0:T(8,128)} %broadcast_in_dim.375), calls=%async_computation.16 | async-start | bytes 1048576 | tf_op jit(solution)/shard_map/all_to_all | solution.py:107
  372.9 13.1 %all-to-all-start.17 = ((f32[8,32,512]{2,1,0:T(8,128)}), f32[8,32,512]{2,1,0:T(8,128)S(1)}, u32[]{:S(2)}, u32[]{:S(2)}) async-start(f32[8,32,512]{2,1,0:T(8,128)} %copy-done.46), calls=%async_computation.17 | async-start | bytes 1048576 | tf_op jit(solution)/shard_map/all_to_all | solution.py:107
  391.6 5.9 collective-permute-start.8
  398.3 13.1 %all-to-all-start.18 = ((f32[8,32,512]{2,1,0:T(8,128)}), f32[8,32,512]{2,1,0:T(8,128)S(1)}, u32[]{:S(2)}, u32[]{:S(2)}) async-start(f32[8,32,512]{2,1,0:T(8,128)} %broadcast_in_dim.378), calls=%async_computation.18 | async-start | bytes 1048576 | tf_op jit(solution)/shard_map/all_to_all | solution.py:107
  417.8 13.1 %all-to-all-start.19 = ((f32[8,32,512]{2,1,0:T(8,128)}), f32[8,32,512]{2,1,0:T(8,128)S(1)}, u32[]{:S(2)}, u32[]{:S(2)}) async-start(f32[8,32,512]{2,1,0:T(8,128)} %shard_map.86), calls=%async_computation.19 | async-start | bytes 1048576 | tf_op jit(solution)/shard_map/all_to_all | solution.py:107
  436.5 5.9 collective-permute-start.9
  443.3 13.1 %all-to-all-start.20 = ((f32[8,32,512]{2,1,0:T(8,128)}), f32[8,32,512]{2,1,0:T(8,128)S(1)}, u32[]{:S(2)}, u32[]{:S(2)}) async-start(f32[8,32,512]{2,1,0:T(8,128)} %broadcast_in_dim.381), calls=%async_computation.20 | async-start | bytes 1048576 | tf_op jit(solution)/shard_map/all_to_all | solution.py:107
  462.8 13.1 %all-to-all-start.21 = ((f32[8,32,512]{2,1,0:T(8,128)}), f32[8,32,512]{2,1,0:T(8,128)S(1)}, u32[]{:S(2)}, u32[]{:S(2)}) async-start(f32[8,32,512]{2,1,0:T(8,128)} %shard_map.88), calls=%async_computation.21 | async-start | bytes 1048576 | tf_op jit(solution)/shard_map/all_to_all | solution.py:107
  481.5 5.9 collective-permute-start.10
  488.2 13.1 %all-to-all-start.22 = ((f32[8,32,512]{2,1,0:T(8,128)}), f32[8,32,512]{2,1,0:T(8,128)S(1)}, u32[]{:S(2)}, u32[]{:S(2)}) async-start(f32[8,32,512]{2,1,0:T(8,128)} %broadcast_in_dim.384), calls=%async_computation.22 | async-start | bytes 1048576 | tf_op jit(solution)/shard_map/all_to_all | solution.py:107
  507.7 13.3 %all-to-all-start.23 = ((f32[8,32,512]{2,1,0:T(8,128)}), f32[8,32,512]{2,1,0:T(8,128)S(1)}, u32[]{:S(2)}, u32[]{:S(2)}) async-start(f32[8,32,512]{2,1,0:T(8,128)} %shard_map.90), calls=%async_computation.23 | async-start | bytes 1048576 | tf_op jit(solution)/shard_map/all_to_all | solution.py:107
  526.7 5.9 collective-permute-start.11
  533.4 13.1 %all-to-all-start.24 = ((f32[8,32,512]{2,1,0:T(8,128)}), f32[8,32,512]{2,1,0:T(8,128)S(1)}, u32[]{:S(2)}, u32[]{:S(2)}) async-start(f32[8,32,512]{2,1,0:T(8,128)} %broadcast_in_dim.387), calls=%async_computation.24 | async-start | bytes 1048576 | tf_op jit(solution)/shard_map/all_to_all | solution.py:107
  553.0 13.1 %all-to-all-start.25 = ((f32[8,32,512]{2,1,0:T(8,128)}), f32[8,32,512]{2,1,0:T(8,128)S(1)}, u32[]{:S(2)}, u32[]{:S(2)}) async-start(f32[8,32,512]{2,1,0:T(8,128)} %shard_map.92), calls=%async_computation.25 | async-start | bytes 1048576 | tf_op jit(solution)/shard_map/all_to_all | solution.py:107
  571.7 5.9 collective-permute-start.12
  578.4 13.1 %all-to-all-start.26 = ((f32[8,32,512]{2,1,0:T(8,128)}), f32[8,32,512]{2,1,0:T(8,128)S(1)}, u32[]{:S(2)}, u32[]{:S(2)}) async-start(f32[8,32,512]{2,1,0:T(8,128)} %broadcast_in_dim.390), calls=%async_computation.26 | async-start | bytes 1048576 | tf_op jit(solution)/shard_map/all_to_all | solution.py:107
  597.9 13.1 %all-to-all-start.27 = ((f32[8,32,512]{2,1,0:T(8,128)}), f32[8,32,512]{2,1,0:T(8,128)S(1)}, u32[]{:S(2)}, u32[]{:S(2)}) async-start(f32[8,32,512]{2,1,0:T(8,128)} %shard_map.94), calls=%async_computation.27 | async-start | bytes 1048576 | tf_op jit(solution)/shard_map/all_to_all | solution.py:107
  616.6 5.9 collective-permute-start.13
  623.4 13.1 %all-to-all-start.28 = ((f32[8,32,512]{2,1,0:T(8,128)}), f32[8,32,512]{2,1,0:T(8,128)S(1)}, u32[]{:S(2)}, u32[]{:S(2)}) async-start(f32[8,32,512]{2,1,0:T(8,128)} %broadcast_in_dim.393), calls=%async_computation.28 | async-start | bytes 1048576 | tf_op jit(solution)/shard_map/all_to_all | solution.py:107
  642.9 13.1 %all-to-all-start.29 = ((f32[8,32,512]{2,1,0:T(8,128)}), f32[8,32,512]{2,1,0:T(8,128)S(1)}, u32[]{:S(2)}, u32[]{:S(2)}) async-start(f32[8,32,512]{2,1,0:T(8,128)} %shard_map.96), calls=%async_computation.29 | async-start | bytes 1048576 | tf_op jit(solution)/shard_map/all_to_all | solution.py:107
  661.6 5.9 collective-permute-start.14
  668.3 13.1 %all-to-all-start.30 = ((f32[8,32,512]{2,1,0:T(8,128)}), f32[8,32,512]{2,1,0:T(8,128)S(1)}, u32[]{:S(2)}, u32[]{:S(2)}) async-start(f32[8,32,512]{2,1,0:T(8,128)} %broadcast_in_dim.396), calls=%async_computation.30 | async-start | bytes 1048576 | tf_op jit(solution)/shard_map/all_to_all | solution.py:107
  687.8 13.3 %all-to-all-start.31 = ((f32[8,32,512]{2,1,0:T(8,128)}), f32[8,32,512]{2,1,0:T(8,128)S(1)}, u32[]{:S(2)}, u32[]{:S(2)}) async-start(f32[8,32,512]{2,1,0:T(8,128)} %shard_map.98), calls=%async_computation.31 | async-start | bytes 1048576 | tf_op jit(solution)/shard_map/all_to_all | solution.py:107
  706.8 5.9 collective-permute-start.15
  713.5 13.1 %all-to-all-start.32 = ((f32[8,32,512]{2,1,0:T(8,128)}), f32[8,32,512]{2,1,0:T(8,128)S(1)}, u32[]{:S(2)}, u32[]{:S(2)}) async-start(f32[8,32,512]{2,1,0:T(8,128)} %broadcast_in_dim.399), calls=%async_computation.32 | async-start | bytes 1048576 | tf_op jit(solution)/shard_map/all_to_all | solution.py:107
  733.0 13.1 %all-to-all-start.33 = ((f32[8,32,512]{2,1,0:T(8,128)}), f32[8,32,512]{2,1,0:T(8,128)S(1)}, u32[]{:S(2)}, u32[]{:S(2)}) async-start(f32[8,32,512]{2,1,0:T(8,128)} %shard_map.100), calls=%async_computation.33 | async-start | bytes 1048576 | tf_op jit(solution)/shard_map/all_to_all | solution.py:107
  751.7 5.9 collective-permute-start.16
  758.4 13.1 %all-to-all-start.34 = ((f32[8,32,512]{2,1,0:T(8,128)}), f32[8,32,512]{2,1,0:T(8,128)S(1)}, u32[]{:S(2)}, u32[]{:S(2)}) async-start(f32[8,32,512]{2,1,0:T(8,128)} %broadcast_in_dim.402), calls=%async_computation.34 | async-start | bytes 1048576 | tf_op jit(solution)/shard_map/all_to_all | solution.py:107
  777.9 13.1 %all-to-all-start.35 = ((f32[8,32,512]{2,1,0:T(8,128)}), f32[8,32,512]{2,1,0:T(8,128)S(1)}, u32[]{:S(2)}, u32[]{:S(2)}) async-start(f32[8,32,512]{2,1,0:T(8,128)} %shard_map.102), calls=%async_computation.35 | async-start | bytes 1048576 | tf_op jit(solution)/shard_map/all_to_all | solution.py:107
  796.6 5.9 collective-permute-start.17
  803.4 13.1 %all-to-all-start.36 = ((f32[8,32,512]{2,1,0:T(8,128)}), f32[8,32,512]{2,1,0:T(8,128)S(1)}, u32[]{:S(2)}, u32[]{:S(2)}) async-start(f32[8,32,512]{2,1,0:T(8,128)} %broadcast_in_dim.405), calls=%async_computation.36 | async-start | bytes 1048576 | tf_op jit(solution)/shard_map/all_to_all | solution.py:107
  822.9 13.1 %all-to-all-start.37 = ((f32[8,32,512]{2,1,0:T(8,128)}), f32[8,32,512]{2,1,0:T(8,128)S(1)}, u32[]{:S(2)}, u32[]{:S(2)}) async-start(f32[8,32,512]{2,1,0:T(8,128)} %shard_map.104), calls=%async_computation.37 | async-start | bytes 1048576 | tf_op jit(solution)/shard_map/all_to_all | solution.py:107
  (62 other events, 321.1 us)
